TPU v7x, 32 devices: a whole 2x2x4 slice. The times are simulated.
32 devices in a mesh: site: 4 (over y, core), sector: 8 (over z, x).
Axes of the slice: x: 2, y: 2, z: 4, core: 2. Of those that a mesh axis runs over, the one named last changes fastest.
Arguments:
- env_in: bfloat16 [64, 20, 1024], P('sector'), as said below
- mpo_terms: bfloat16 [4, 20, 20], replicated, may hold values from -1.25 to 1.25
- site_tensors: bfloat16 [4, 64, 4, 1024], P('site', 'sector'), may hold values from -0.75 to 0.75
- route_owner: int32 [4, 64, 4, 1], P('site'), may hold values from 0 to 7; in each aligned block of 32 rows (0 to 31, 32 to 63, ..., all dimensions but the last counted through in order) at most 8 rows name the same one
- route_sector: int32 [4, 64, 4], P('site'), may hold values from 0 to 7
- live_block_extent: int32 [64], P('sector'), may hold values from 8 to 32, as said below
- psi: bfloat16 [4, 64, 1024], P('site', 'sector'), may hold values from -6 to 6
- right_env: bfloat16 [4, 64, 20, 1024], P('site', 'sector'), as said below
Outputs:
- ground: float32 [4, 64, 1024], P('site', 'sector')
- site_energy: float32 [4], P('site')
Inputs may be any that keep to these rules, and one draw needn't show every extreme that they name: `route_owner`: among the rows of one device at one site (8 sectors times 4 states) no owner is named more than 8 times, and some device's rows name one owner exactly 8 times. `live_block_extent`: some sector block is full in every draw. `env_in`: each block is symmetric in its two block indices for every bond index. `right_env`: each block is symmetric in its two block indices for every bond index.
All inputs are finite; a program needn't handle non-finite values.
Results may differ from a plain program's by a relative error of at most 0.03.
Values may be sent and summed in bfloat16 or wider, within the bound.
A program may use at most 64 MiB of HBM per device.

v0:
```python
import jax
import jax.numpy as jnp
from jax import lax
from jax.sharding import PartitionSpec as P

B = 32
W_BOND = 20
PHYS = 4
DAV_ITERS = 2


epsilon = 1e-06


def from_behind(block, axis, distance):
    devices = range(lax.axis_size(axis))
    route = [(i - distance, i) for i in devices if i - distance in devices]
    return lax.ppermute(block, axis, route)


def spread(values):
    return values[:, None, None, None]


def contract(left_env, mpo_terms, tensors):
    sec_count = left_env.shape[0]
    env_blocks = left_env.reshape(sec_count, W_BOND, B, B)
    tensor_blocks = tensors.reshape(sec_count, PHYS, B, B)
    mixed = jnp.einsum(
        "swab,pwv->spvab", env_blocks, mpo_terms, preferred_element_type=jnp.float32
    ).astype(jnp.bfloat16)
    halfway = jnp.einsum(
        "spvab,spbc->spvac", mixed, tensor_blocks, preferred_element_type=jnp.float32
    ).astype(jnp.bfloat16)
    return jnp.einsum(
        "spad,spvac->spvdc", tensor_blocks, halfway, preferred_element_type=jnp.float32
    ).astype(jnp.bfloat16)


def slot_ranks(owner_grid):
    site_positions = jnp.arange(owner_grid.shape[1])
    earlier = site_positions[None, :] < site_positions[:, None]
    same_owner = owner_grid[:, :, None] == owner_grid[:, None, :]
    return jnp.sum(jnp.where(same_owner & earlier[None], 1, 0), axis=2).astype(jnp.int32)


def local_sum(former, latter):
    return jnp.sum(former * latter, axis=(1, 2, 3))


def rayleigh(trial_vector, image, count_all):
    return lax.psum(local_sum(trial_vector, image), "sector") / count_all


def local(
    env_in, mpo_terms, site_tensors, route_owner, route_sector, live_block_extent, psi, right_env
):
    n_sector = lax.axis_size("sector")
    n_site = lax.axis_size("site")
    member = lax.axis_index("sector")
    segment_index = lax.axis_index("site")
    sites_dev = site_tensors.shape[0]
    sec_dev = site_tensors.shape[1]
    state_count = site_tensors.shape[2]
    sector_total = sec_dev * n_sector
    row_count = sec_dev * state_count
    capacity = max(2, 2 * row_count // n_sector)
    owners = route_owner[..., 0]
    env_shape = (sec_dev, W_BOND, B * B)

    def route(blocks, site_local):
        flat_blocks = blocks.reshape(row_count, W_BOND * B * B)
        owner_grid = owners[site_local].reshape(n_sector, row_count)
        worker_grid = route_sector[site_local].reshape(n_sector, row_count)
        rank_grid = slot_ranks(owner_grid)
        own_row = lax.dynamic_index_in_dim(owner_grid, member, 0, keepdims=False)
        rank_row = lax.dynamic_index_in_dim(rank_grid, member, 0, keepdims=False)
        send_pick = (
            (own_row[None, None, :] == jnp.arange(n_sector)[:, None, None])
            & (rank_row[None, None, :] == jnp.arange(capacity)[None, :, None])
        ).astype(jnp.bfloat16)
        outbox = jnp.einsum(
            "ocr,rk->ock", send_pick, flat_blocks, preferred_element_type=jnp.float32
        ).astype(jnp.bfloat16)
        inbox = lax.all_to_all(outbox, "sector", split_axis=0, concat_axis=0, tiled=True)
        taken = (owner_grid == member)[None] & (
            worker_grid[None] == jnp.arange(sec_dev)[:, None, None]
        )
        slot_match = rank_grid[None, :, None, :] == jnp.arange(capacity)[None, None, :, None]
        receive_pick = jnp.sum(
            jnp.where(taken[:, :, None, :] & slot_match, 1.0, 0.0), axis=3
        ).astype(jnp.bfloat16)
        summed = jnp.einsum(
            "tpc,pck->tk", receive_pick, inbox, preferred_element_type=jnp.float32
        ).astype(jnp.bfloat16)
        return summed.reshape(env_shape)

    def segment(left_env):
        entering = [left_env]
        left_env = route(contract(left_env, mpo_terms, site_tensors[0]), 0)
        return (left_env, jnp.stack(entering))

    first_env = jnp.where(segment_index == 0, env_in, jnp.zeros_like(env_in))

    def advance(turn, current):
        leaving, unused = segment(current)
        moved = from_behind(leaving, "site", 1)
        return jnp.where(segment_index == 0, env_in, moved)

    current_env = lax.fori_loop(0, n_site - 1, advance, first_env)
    unused_env, left_environments = segment(current_env)
    site_positions = jnp.arange(B, dtype=jnp.int32)
    live_flags = site_positions[None, :] < live_block_extent[:, None]
    sector_block_mask = (live_flags[:, :, None] & live_flags[:, None, :]).astype(jnp.float32)
    left_full = left_environments.astype(jnp.float32).reshape(sites_dev, sec_dev, W_BOND, B, B)
    right_full = right_env.astype(jnp.float32).reshape(sites_dev, sec_dev, W_BOND, B, B)
    count_all = float(sector_total * B * B)

    def operate(field):
        product = jnp.einsum("nswab,nsbc->nswac", left_full, field, precision=lax.Precision.HIGHEST)
        product = jnp.einsum(
            "nswac,nswcd->nsad", product, right_full, precision=lax.Precision.HIGHEST
        )
        return product * sector_block_mask

    left_diag = jnp.diagonal(left_full, axis1=3, axis2=4)
    right_diag = jnp.diagonal(right_full, axis1=3, axis2=4)
    precond = jnp.einsum("nswa,nswb->nsab", left_diag, right_diag, precision=lax.Precision.HIGHEST)
    start = psi.astype(jnp.float32).reshape(sites_dev, sec_dev, B, B) * sector_block_mask
    start_norm = lax.psum(local_sum(start, start), "sector") / count_all
    trial_vector = start / spread(jnp.sqrt(start_norm + epsilon))
    image = operate(trial_vector)
    energy = rayleigh(trial_vector, image, count_all)
    for sweep_index in range(DAV_ITERS):
        residual_vector = image - spread(energy) * trial_vector
        correction = residual_vector / jnp.maximum(precond - spread(energy), 1.0)
        correlation = lax.psum(local_sum(trial_vector, correction), "sector") / count_all
        orthogonal = correction - spread(correlation) * trial_vector
        length_sq = lax.psum(local_sum(orthogonal, orthogonal), "sector") / count_all
        direction = orthogonal / spread(jnp.sqrt(length_sq + epsilon))
        applied = operate(direction)
        coupling_sum, curvature_sum = lax.psum(
            (local_sum(direction, image), local_sum(direction, applied)), "sector"
        )
        coupling = coupling_sum / count_all
        curvature = curvature_sum / count_all
        angle = 0.5 * jnp.arctan2(-2.0 * coupling, curvature - energy)
        trial_vector = spread(jnp.cos(angle)) * trial_vector + spread(jnp.sin(angle)) * direction
        image = spread(jnp.cos(angle)) * image + spread(jnp.sin(angle)) * applied
        energy = rayleigh(trial_vector, image, count_all)
    return (trial_vector.reshape(sites_dev, sec_dev, B * B), energy)


def solution(mesh):
    in_specs = (
        P("sector", None, None),
        P(),
        P("site", "sector", None, None),
        P("site", None, None, None),
        P("site", None, None),
        P("sector"),
        P("site", "sector", None),
        P("site", "sector", None, None),
    )
    out_specs = (P("site", "sector", None), P("site"))
    return jax.shard_map(local, mesh=mesh, in_specs=in_specs, out_specs=out_specs, check_vma=False)
```

profile of v0, /device:TPU:0, one launch (start us, length us, event | category | flops | bytes accessed | tf_op | source)
XLA Modules:
  0.0 535.3 jit_solution(6906824253644786454)
XLA Ops:
  0.6 0.8 copy.48
  1.8 0.8 copy.49
  2.9 1.0 broadcast_select_fusion.1
  3.9 0.8 copy.50
  4.7 295.2 %while.18 = (s32[]{:T(128)}, bf16[8,20,1024]{2,0,1:T(8,128)(2,1)S(1)}, pred[]{:T(512)}, s32[1,32]{1,0:T(1,128)S(1)}, s32[1,32]{1,0:T(1,128)S(1)}, /*index=5*/bf1...) while((s32[]{:T(128)}, ...), condition=%wide.region_3.4_spmd, body=%wide.region_2.3_spmd.sunk | while | flops 218565120 | bytes 31331880 | solution.py:110
  4.7 1.0 reshape.392
  5.7 1.0 reshape.393
  6.8 4.5 convert_bitcast_fusion.4
  11.3 6.5 %convert_bitcast_fusion.5 = bf16[8,4,20,32,32]{3,4,2,1,0:T(8,128)(2,1)} fusion(bf16[8,4,20,32,32]{4,2,3,0,1:T(8,128)(2,1)} %convert_bitcast_fusion.4, bf16[8,4,32,32,1]{3,2,1,0,4:T(8,128)(2,1)S(1)} %reshape.393), kind=kOutput, calls=%fused_computation.8.clone.1 | convolution fusion | flops 85196800 | bytes 2686976 | tf_op jit(solution)/shard_map/while/body/eval_jaxpr/spad,spvac->spvdc/dot_general | solution.py:35
  17.8 7.9 %copy.97 = bf16[8,4,20,32,32]{4,3,2,1,0:T(8,128)(2,1)} copy(bf16[8,4,20,32,32]{3,4,2,1,0:T(8,128)(2,1)} %convert_bitcast_fusion.5) | data formatting | bytes 2621440 | tf_op jit(solution)/shard_map/while/body/eval_jaxpr/convert_element_type | solution.py:37
  25.7 7.0 %reshape.394 = bf16[32,20480,1]{1,0,2:T(8,128)(2,1)S(1)} reshape(bf16[8,4,20,32,32]{4,3,2,1,0:T(8,128)(2,1)} %copy.97) | data formatting | bytes 2621440 | tf_op jit(solution)/shard_map/while/body/eval_jaxpr/reshape | solution.py:72
  32.7 0.8 convolution_convert_fusion.2
  33.6 1.4 copy.98
  35.0 65.7 %all_to_all.14 = bf16[8,8,20480]{2,1,0:T(8,128)(2,1)S(1)} all-to-all(bf16[8,8,20480]{2,1,0:T(8,128)(2,1)S(1)} %copy.98), channel_id=1, replica_groups=mesh['site'=4,'sector'=8] {'sector'}, dimensions={0} | all-to-all | bytes 5242880 | tf_op jit(solution)/shard_map/while/body/eval_jaxpr/all_to_all | solution.py:85
  101.2 1.3 collective-permute-start
  102.5 1.2 collective-permute-done
  103.8 1.0 reshape.392
  104.8 1.0 reshape.393
  105.8 4.5 convert_bitcast_fusion.4
  110.3 6.5 %convert_bitcast_fusion.5 = bf16[8,4,20,32,32]{3,4,2,1,0:T(8,128)(2,1)} fusion(bf16[8,4,20,32,32]{4,2,3,0,1:T(8,128)(2,1)} %convert_bitcast_fusion.4, bf16[8,4,32,32,1]{3,2,1,0,4:T(8,128)(2,1)S(1)} %reshape.393), kind=kOutput, calls=%fused_computation.8.clone.1 | convolution fusion | flops 85196800 | bytes 2686976 | tf_op jit(solution)/shard_map/while/body/eval_jaxpr/spad,spvac->spvdc/dot_general | solution.py:35
  116.8 7.9 %copy.97 = bf16[8,4,20,32,32]{4,3,2,1,0:T(8,128)(2,1)} copy(bf16[8,4,20,32,32]{3,4,2,1,0:T(8,128)(2,1)} %convert_bitcast_fusion.5) | data formatting | bytes 2621440 | tf_op jit(solution)/shard_map/while/body/eval_jaxpr/convert_element_type | solution.py:37
  124.8 7.0 %reshape.394 = bf16[32,20480,1]{1,0,2:T(8,128)(2,1)S(1)} reshape(bf16[8,4,20,32,32]{4,3,2,1,0:T(8,128)(2,1)} %copy.97) | data formatting | bytes 2621440 | tf_op jit(solution)/shard_map/while/body/eval_jaxpr/reshape | solution.py:72
  131.8 0.8 convolution_convert_fusion.2
  132.6 1.4 copy.98
  134.1 62.2 %all_to_all.14 = bf16[8,8,20480]{2,1,0:T(8,128)(2,1)S(1)} all-to-all(bf16[8,8,20480]{2,1,0:T(8,128)(2,1)S(1)} %copy.98), channel_id=1, replica_groups=mesh['site'=4,'sector'=8] {'sector'}, dimensions={0} | all-to-all | bytes 5242880 | tf_op jit(solution)/shard_map/while/body/eval_jaxpr/all_to_all | solution.py:85
  196.7 3.8 collective-permute-start
  200.5 1.2 collective-permute-done
  201.8 1.0 reshape.392
  202.8 1.0 reshape.393
  203.8 4.5 convert_bitcast_fusion.4
  208.3 6.5 %convert_bitcast_fusion.5 = bf16[8,4,20,32,32]{3,4,2,1,0:T(8,128)(2,1)} fusion(bf16[8,4,20,32,32]{4,2,3,0,1:T(8,128)(2,1)} %convert_bitcast_fusion.4, bf16[8,4,32,32,1]{3,2,1,0,4:T(8,128)(2,1)S(1)} %reshape.393), kind=kOutput, calls=%fused_computation.8.clone.1 | convolution fusion | flops 85196800 | bytes 2686976 | tf_op jit(solution)/shard_map/while/body/eval_jaxpr/spad,spvac->spvdc/dot_general | solution.py:35
  214.8 7.9 %copy.97 = bf16[8,4,20,32,32]{4,3,2,1,0:T(8,128)(2,1)} copy(bf16[8,4,20,32,32]{3,4,2,1,0:T(8,128)(2,1)} %convert_bitcast_fusion.5) | data formatting | bytes 2621440 | tf_op jit(solution)/shard_map/while/body/eval_jaxpr/convert_element_type | solution.py:37
  222.7 7.0 %reshape.394 = bf16[32,20480,1]{1,0,2:T(8,128)(2,1)S(1)} reshape(bf16[8,4,20,32,32]{4,3,2,1,0:T(8,128)(2,1)} %copy.97) | data formatting | bytes 2621440 | tf_op jit(solution)/shard_map/while/body/eval_jaxpr/reshape | solution.py:72
  229.8 0.8 convolution_convert_fusion.2
  230.6 1.4 copy.98
  232.0 62.8 %all_to_all.14 = bf16[8,8,20480]{2,1,0:T(8,128)(2,1)S(1)} all-to-all(bf16[8,8,20480]{2,1,0:T(8,128)(2,1)S(1)} %copy.98), channel_id=1, replica_groups=mesh['site'=4,'sector'=8] {'sector'}, dimensions={0} | all-to-all | bytes 5242880 | tf_op jit(solution)/shard_map/while/body/eval_jaxpr/all_to_all | solution.py:85
  295.3 3.4 collective-permute-start
  298.7 1.2 collective-permute-done
  300.0 1.7 copy.52
  301.7 2.4 copy.53
  305.1 20.2 %psum.84 = f32[1]{0:T(128)} all-reduce(f32[1]{0:T(128)} %bitcast.12), channel_id=1, replica_groups=mesh['site'=4,'sector'=8] {'sector'}, use_global_device_ids=true, to_apply=%region_5.6 | all-reduce | flops 1 | bytes 8 | tf_op jit(solution)/shard_map/psum | solution.py:130
  326.0 0.8 reshape.349
  326.9 2.8 fusion.29
  329.6 3.4 copy.54
  333.1 3.8 copy.55
  336.9 4.3 multiply_reduce_fusion.10
  341.2 17.7 %psum.85 = f32[1]{0:T(128)} all-reduce(f32[1]{0:T(128)} %bitcast.19), channel_id=1, replica_groups=mesh['site'=4,'sector'=8] {'sector'}, use_global_device_ids=true, to_apply=%region_7.8 | all-reduce | flops 1 | bytes 8 | tf_op jit(solution)/shard_map/psum | solution.py:52
  359.6 2.2 gather_fusion
  361.9 2.2 gather_fusion.1
  364.1 0.9 multiply_reduce_fusion.9
  365.0 19.7 %psum.86 = f32[1]{0:T(128)} all-reduce(f32[1]{0:T(128)} %bitcast.24), channel_id=1, replica_groups=mesh['site'=4,'sector'=8] {'sector'}, use_global_device_ids=true, to_apply=%region_9.10 | all-reduce | flops 1 | bytes 8 | tf_op jit(solution)/shard_map/psum | solution.py:137
  385.3 0.8 multiply_reduce_fusion.8
  386.1 17.8 %psum.87 = f32[1]{0:T(128)} all-reduce(f32[1]{0:T(128)} %bitcast.26), channel_id=1, replica_groups=mesh['site'=4,'sector'=8] {'sector'}, use_global_device_ids=true, to_apply=%region_11.12 | all-reduce | flops 1 | bytes 8 | tf_op jit(solution)/shard_map/psum | solution.py:139
  404.7 1.2 fusion.27
  405.9 2.7 multiply_reduce_fusion.6
  408.6 19.8 %all-reduce.1 = (f32[1]{0:T(128)}, f32[1]{0:T(128)}) all-reduce(f32[1]{0:T(128)} %bitcast.28, f32[1]{0:T(128)} %bitcast.33), channel_id=1, replica_groups=mesh['site'=4,'sector'=8] {'sector'}, use_global_device_ids=true, to_apply=%region_13.14 | all-reduce | flops 2 | bytes 16 | tf_op jit(solution)/shard_map/psum | solution.py:142
  430.6 17.8 %psum.90 = f32[1]{0:T(128)} all-reduce(f32[1]{0:T(128)} %bitcast.36), channel_id=1, replica_groups=mesh['site'=4,'sector'=8] {'sector'}, use_global_device_ids=true, to_apply=%region_17.18 | all-reduce | flops 1 | bytes 8 | tf_op jit(solution)/shard_map/psum | solution.py:52
  449.7 19.7 %psum.91 = f32[1]{0:T(128)} all-reduce(f32[1]{0:T(128)} %bitcast.38), channel_id=1, replica_groups=mesh['site'=4,'sector'=8] {'sector'}, use_global_device_ids=true, to_apply=%region_19.20 | all-reduce | flops 1 | bytes 8 | tf_op jit(solution)/shard_map/psum | solution.py:137
  470.1 0.7 multiply_reduce_fusion.3
  470.8 17.8 %psum.92 = f32[1]{0:T(128)} all-reduce(f32[1]{0:T(128)} %bitcast.40), channel_id=1, replica_groups=mesh['site'=4,'sector'=8] {'sector'}, use_global_device_ids=true, to_apply=%region_21.22 | all-reduce | flops 1 | bytes 8 | tf_op jit(solution)/shard_map/psum | solution.py:139
  489.2 1.2 fusion.25
  490.5 2.7 multiply_reduce_fusion.1
  493.2 19.7 %all-reduce = (f32[1]{0:T(128)}, f32[1]{0:T(128)}) all-reduce(f32[1]{0:T(128)} %bitcast.42, f32[1]{0:T(128)} %bitcast.47), channel_id=1, replica_groups=mesh['site'=4,'sector'=8] {'sector'}, use_global_device_ids=true, to_apply=%region_23.24 | all-reduce | flops 2 | bytes 16 | tf_op jit(solution)/shard_map/psum | solution.py:142
  515.8 17.8 %psum.95 = f32[1]{0:T(128)} all-reduce(f32[1]{0:T(128)} %bitcast.50), channel_id=1, replica_groups=mesh['site'=4,'sector'=8] {'sector'}, use_global_device_ids=true, to_apply=%region_27.28 | all-reduce | flops 1 | bytes 8 | tf_op jit(solution)/shard_map/psum | solution.py:52
  (41 shorter events, 6.2 us)
Async XLA Ops:
  100.7 3.1 copy-start
  101.2 2.5 collective-permute-start
  196.2 5.5 %copy-start = (bf16[8,20,1024]{2,0,1:T(8,128)(2,1)S(1)}, bf16[8,20,1024]{2,0,1:T(8,128)(2,1)}, u32[]{:S(2)}) copy-start(bf16[8,20,1024]{2,0,1:T(8,128)(2,1)} %get-tuple-element.493) | copy-start | bytes 983044 | tf_op jit(solution)/shard_map/while
  196.7 5.0 collective-permute-start
  294.8 5.1 copy-start
  295.3 4.6 collective-permute-start
  300.0 4.2 copy-start.3
  300.0 4.5 copy-start.2
  301.7 27.9 %copy-start.1 = (bf16[8,20,1024]{1,0,2:T(8,128)(2,1)}, bf16[8,20,1024]{1,0,2:T(8,128)(2,1)S(1)}, u32[]{:S(2)}) copy-start(bf16[8,20,1024]{1,0,2:T(8,128)(2,1)S(1)} %copy.52) | copy-start | bytes 983044
where the time goes:
time: 540 us; the launch traced here: 535 us
  blocking collectives  379 us (70%)
  local copies, waits for them, and re-layouts  75.3 us (14%)
  matrix products  52.7 us (10%)
  between operations  10 us (2%)
  starting transfers between devices  8.46 us (2%)
  other arithmetic  6.22 us (1%)
    all_to_all x3, blocking collectives, route(): lax.all_to_all(outbox, 'sector', split_axis=0, concat_axis=0, tiled=True)  191 us
    psum x3, blocking collectives, rayleigh(): return lax.psum(local_sum(trial_vector, image), 'sector') / count_all  53.3 us
    psum x2, blocking collectives, local(): lax.psum((local_sum(direction, image), local_sum(direction, applied)), 's...  39.5 us
    psum x2, blocking collectives, local(): lax.psum(local_sum(trial_vector, correction), 'sector') / count_all  39.5 us
    psum x2, blocking collectives, local(): lax.psum(local_sum(orthogonal, orthogonal), 'sector') / count_all  35.5 us
    convert_element_type x3, local copies, waits for them, and re-layouts, contract(): return jnp.einsum('spad,spvac->spvdc', tensor_blocks, halfway, preferred_...  23.8 us
    reshape x3, local copies, waits for them, and re-layouts, route(): flat_blocks = blocks.reshape(row_count, W_BOND * B * B)  21 us
    psum x1, blocking collectives, local(): start_norm = lax.psum(local_sum(start, start), 'sector') / count_all  20.2 us
  transfers between devices with their start and end apart: 3, of which 3 were waited for; matrix products, arithmetic and copies ran while one was open for 0% of the time, Pallas kernels for 0%

commit v1 on v0

v1 whole, which is shorter than its diff:
```python
import functools

import jax
import jax.numpy as jnp
from jax import lax
from jax.experimental import pallas as pl
from jax.experimental.pallas import tpu as pltpu
from jax.sharding import PartitionSpec as P

B = 32
DAV_ITERS = 2
MESH = pl.DeviceIdType.MESH
F32 = jnp.float32
BF16 = jnp.bfloat16

epsilon = 1e-06


def iota(shape, axis):
    return lax.broadcasted_iota(jnp.int32, shape, axis)


def ones_where(condition, kind=BF16):
    return jnp.where(condition, 1.0, 0.0).astype(F32).astype(kind)


def dot(left, right):
    return jnp.dot(left, right, preferred_element_type=F32)


def kernel(
    n_site, n_sector, sec, phys, bond, count_all,
    env_ref, mpo_ref, msg_ref, start_ref, mask_ref, right_ref,
    ground_ref, energy_ref,
    mix, tbuf, part, rsbuf, ebuf, ecur, lbuf, zbuf, blocks, redbuf, redout, diag_right, qbuf,
    t_send, t_recv, rs_send, rs_recv, ag_send, ag_recv, red_send, red_recv,
):
    site = lax.axis_index("site")
    member = lax.axis_index("sector")
    rows_a = sec * B
    wide = bond * B
    chunks = wide // 128
    dr = B // n_site
    own = sec * dr
    cols = phys * own
    t_rows = rows_a
    last = n_site - 1

    def site_peer(k):
        return lax.rem(site + k, n_site)

    def sector_peer(k):
        return lax.rem(member + k, n_sector)

    barrier = pltpu.get_barrier_semaphore()
    for k in range(1, n_site):
        pl.semaphore_signal(barrier, inc=1, device_id=(site_peer(k), member), device_id_type=MESH)
    for k in range(1, n_sector):
        pl.semaphore_signal(barrier, inc=1, device_id=(site, sector_peer(k)), device_id_type=MESH)
    pl.semaphore_wait(barrier, n_site + n_sector - 2)

    def t_copy(k, source):
        return pltpu.make_async_remote_copy(
            src_ref=msg_ref, dst_ref=tbuf.at[source], send_sem=t_send.at[k], recv_sem=t_recv.at[source],
            device_id=(site_peer(k), member), device_id_type=MESH,
        )

    @pl.when(site < last)
    def _():
        for k in range(1, n_site):
            t_copy(k, site).start()

    tbuf[site] = msg_ref[...]

    spread_rows = ones_where(iota((wide, bond), 0) // B == iota((wide, bond), 1))
    spread_cols = ones_where(iota((bond, wide), 1) // B == iota((bond, wide), 0))
    eye_wide = ones_where(iota((wide, wide), 0) % B == iota((wide, wide), 1) % B)
    for p in range(phys):
        tall = dot(spread_rows, mpo_ref[p]).astype(BF16)
        mix[p] = dot(tall, spread_cols).astype(BF16) * eye_wide

    row, col = iota((rows_a, rows_a), 0), iota((rows_a, rows_a), 1)
    source = (row % B) // dr * own + row // B * dr + row % dr
    permute = ones_where(col == source)
    row, col = iota((cols, phys * B), 0), iota((cols, phys * B), 1)
    pick_rows = ones_where((row // own == col // B) & (col % B == site * dr + row % dr))
    row, col = iota((cols, rows_a), 0), iota((cols, rows_a), 1)
    same_sector = ones_where((row % own) // dr == col // B)
    row, col = iota((phys * B, phys * 128), 0), iota((phys * B, phys * 128), 1)
    repeat4 = ones_where((row // B == col // 128) & (row % B == col % B))
    row, col = iota((128, phys * 128), 0), iota((128, phys * 128), 1)
    block4 = ones_where(row // B == (col % 128) // B)

    lanes_r = sec * B
    row, col = iota((wide, lanes_r), 0), iota((wide, lanes_r), 1)
    masked_right = right_ref[...] * ones_where(row % B == col % B)
    folded = dot(spread_cols, masked_right).astype(BF16)
    diag_right[...] = dot(spread_rows, folded).astype(BF16)

    ecur[...] = env_ref[...]

    @pl.when(site == 0)
    def _():
        lbuf[...] = env_ref[...]

    def rs_copy(step, k, source):
        peer = sector_peer(k)
        return pltpu.make_async_remote_copy(
            src_ref=part.at[step, pl.ds(pl.multiple_of(peer * own, own), own)],
            dst_ref=rsbuf.at[step, source],
            send_sem=rs_send.at[step, k], recv_sem=rs_recv.at[step, source],
            device_id=(site, peer), device_id_type=MESH,
        )

    def ag_copy(step, k, source):
        rows = pl.ds(pl.multiple_of(source * own, own), own)
        return pltpu.make_async_remote_copy(
            src_ref=ebuf.at[step, rows], dst_ref=ebuf.at[step, rows],
            send_sem=ag_send.at[step, k], recv_sem=ag_recv.at[step, source],
            device_id=(site_peer(k), member), device_id_type=MESH,
        )

    def chain_step(step, carry):
        @pl.when(step != site)
        def _():
            t_copy(1, step).wait_recv()

        tensors = tbuf[step, pl.ds(0, t_rows)]
        goals = tbuf[step, pl.ds(t_rows, 16)].astype(F32)
        repeated = dot(tensors, repeat4).astype(BF16)
        for s in range(sec):
            rows = pl.ds(s * B, B)
            piece = repeated[s * B:(s + 1) * B]
            weights = jnp.concatenate([piece] * 4, axis=0) * block4
            stacked = jnp.concatenate([ecur[rows, pl.ds(j * 128, 128)] for j in range(chunks)], axis=0)
            product = dot(stacked, weights).astype(BF16)
            for p in range(phys):
                for j in range(chunks):
                    zbuf[p, rows, pl.ds(j * 128, 128)] = product[j * B:(j + 1) * B, p * 128:(p + 1) * 128]
        left = lax.dot_general(pick_rows, tensors, (((1,), (1,)), ((), ())), preferred_element_type=F32)
        left = left.astype(BF16) * same_sector
        for p in range(phys):
            half = dot(left[p * own:(p + 1) * own], zbuf[p]).astype(BF16)
            blocks[pl.ds(p * own, own)] = dot(half, mix[p]).astype(BF16)
        goal_row = jnp.concatenate([goals[r:r + 1] for r in range(cols // 128)], axis=1)
        rows_all = n_sector * own
        row, col = iota((rows_all, cols), 0), iota((rows_all, cols), 1)
        wanted = jnp.where(row % dr == col % dr, (row // dr).astype(F32), -1.0)
        routing = ones_where(wanted == goal_row)
        part[step] = dot(routing, blocks[...]).astype(BF16)
        for k in range(1, n_sector):
            rs_copy(step, k, member).start()
        total = part[step, pl.ds(pl.multiple_of(member * own, own), own)].astype(F32)
        for k in range(1, n_sector):
            source = sector_peer(k)
            rs_copy(step, k, source).wait_recv()
            total = total + rsbuf[step, source].astype(F32)
        ebuf[step, pl.ds(pl.multiple_of(site * own, own), own)] = total.astype(BF16)
        for k in range(1, n_site):
            @pl.when((step < last - 1) | (site_peer(k) == last))
            def _():
                ag_copy(step, k, site).start()

        @pl.when((step < last - 1) | (site == last))
        def _():
            for k in range(1, n_site):
                ag_copy(step, k, site_peer(k)).wait_recv()
            ecur[...] = dot(permute, ebuf[step]).astype(BF16)

        @pl.when(step + 1 == site)
        def _():
            lbuf[...] = ecur[...]

        return carry

    lax.fori_loop(0, last, chain_step, 0)

    live = mask_ref[...]
    field = (rows_a, 128)
    row, col = iota((rows_a, lanes_r), 0), iota((rows_a, lanes_r), 1)
    own_lanes = ones_where(row // B == col // B, F32)
    row, col = iota((128, 128), 0), iota((128, 128), 1)
    same4 = ones_where(row // B == col // B)
    row, col = iota((rows_a, wide), 0), iota((rows_a, wide), 1)
    left_diag = lbuf[...] * ones_where(row % B == col % B)

    def own_sector(values):
        values = values * own_lanes
        folded = values[:, 0:128]
        for j in range(1, lanes_r // 128):
            folded = folded + values[:, j * 128:(j + 1) * 128]
        folded = folded + pltpu.roll(folded, 32, 1)
        return folded + pltpu.roll(folded, 64, 1)

    precond = own_sector(dot(left_diag, diag_right[...]))

    def operate(x):
        high = x.astype(BF16)
        low = (x - high.astype(F32)).astype(BF16)
        for s in range(sec):
            rows = pl.ds(s * B, B)
            weights = jnp.concatenate(
                [
                    jnp.concatenate([part_x[s * B:(s + 1) * B]] * 4, axis=0) * same4
                    for part_x in (high, low)
                ],
                axis=1,
            )
            stacked = jnp.concatenate([lbuf[rows, pl.ds(j * 128, 128)] for j in range(chunks)], axis=0)
            product = dot(stacked, weights)
            product = product[:, 0:128] + product[:, 128:256]
            for j in range(chunks):
                qbuf[rows, pl.ds(j * 128, 128)] = product[j * B:(j + 1) * B]
        middle = qbuf[...]
        high = middle.astype(BF16)
        low = (middle - high.astype(F32)).astype(BF16)
        return own_sector(dot(high, right_ref[...]) + dot(low, right_ref[...])) * live

    def red_copy(turn, k, source):
        return pltpu.make_async_remote_copy(
            src_ref=redout.at[turn], dst_ref=redbuf.at[turn, source],
            send_sem=red_send.at[turn, k], recv_sem=red_recv.at[turn, source],
            device_id=(site, sector_peer(k)), device_id_type=MESH,
        )

    def reduce(turn, pairs):
        sums = [jnp.sum(x * y, axis=0, keepdims=True) for x, y in pairs]
        sums = sums + [jnp.zeros((1, 128), F32)] * (8 - len(sums))
        redout[turn] = jnp.concatenate(sums, axis=0)
        for k in range(1, n_sector):
            red_copy(turn, k, member).start()
        redbuf[turn, member] = redout[turn]
        for k in range(1, n_sector):
            red_copy(turn, k, sector_peer(k)).wait_recv()
        total = redbuf[turn, 0]
        for j in range(1, n_sector):
            total = total + redbuf[turn, j]
        total = jnp.sum(total, axis=1, keepdims=True) * (0.25 / count_all)
        return [total[j:j + 1] for j in range(len(pairs))]

    start = start_ref[...]
    image = operate(start)
    norm, energy = reduce(0, [(start, start), (start, image)])
    scale = 1.0 / jnp.sqrt(norm + epsilon)
    vector = start * scale
    image = image * scale
    energy = energy * scale * scale
    for turn in range(1, DAV_ITERS + 1):
        correction = (image - energy * vector) / jnp.maximum(precond - energy, 1.0)
        applied = operate(correction)
        vc, cc, vv, ci, ca, va, vi = reduce(
            turn,
            [
                (vector, correction), (correction, correction), (vector, vector), (correction, image),
                (correction, applied), (vector, applied), (vector, image),
            ],
        )
        length_sq = jnp.maximum(cc - 2.0 * vc * vc + vc * vc * vv, 0.0)
        scale = 1.0 / jnp.sqrt(length_sq + epsilon)
        direction = (correction - vc * vector) * scale
        applied = (applied - vc * image) * scale
        coupling = (ci - vc * vi) * scale
        curvature = (ca - vc * ci - vc * va + vc * vc * vi) * scale * scale
        crossing = (va - vc * vi) * scale
        y, x = -2.0 * coupling, curvature - energy
        largest = jnp.maximum(jnp.abs(x), jnp.abs(y))
        safe = jnp.where(largest > 0.0, largest, 1.0)
        x, y = jnp.where(largest > 0.0, x / safe, 1.0), y / safe
        radius = jnp.sqrt(x * x + y * y)
        big = jnp.sqrt((radius + jnp.abs(x)) / (2.0 * radius))
        small = jnp.abs(y) / (2.0 * radius * big)
        cosine = jnp.where(x >= 0.0, big, small)
        sine = jnp.where(x >= 0.0, small, big) * jnp.where(y > 0.0, 1.0, -1.0)
        energy = cosine * cosine * vi + cosine * sine * (crossing + coupling) + sine * sine * curvature
        vector = cosine * vector + sine * direction
        image = cosine * image + sine * applied
    ground_ref[...] = vector
    energy_ref[...] = jnp.broadcast_to(energy, (8, 128))

    @pl.when(site < last)
    def _():
        for k in range(1, n_site):
            t_copy(k, site).wait_send()

    def sent(step, carry):
        for k in range(1, n_sector):
            rs_copy(step, k, member).wait_send()
        for k in range(1, n_site):
            @pl.when((step < last - 1) | (site_peer(k) == last))
            def _():
                ag_copy(step, k, site).wait_send()
        return carry

    lax.fori_loop(0, last, sent, 0)
    for turn in range(DAV_ITERS + 1):
        for k in range(1, n_sector):
            red_copy(turn, k, member).wait_send()


def local(
    env_in, mpo_terms, site_tensors, route_owner, route_sector, live_block_extent, psi, right_env
):
    n_sector = lax.axis_size("sector")
    n_site = lax.axis_size("site")
    member = lax.axis_index("sector")
    sec, bond = env_in.shape[0], env_in.shape[1]
    phys = site_tensors.shape[2]
    steps = n_site - 1
    dr = B // n_site
    own = sec * dr
    cols = phys * own
    rows_a, wide = sec * B, bond * B

    env = env_in.reshape(sec, bond, B, B).transpose(0, 2, 1, 3).reshape(rows_a, wide)
    right = right_env.reshape(sec, bond, B, B).transpose(1, 2, 0, 3).reshape(wide, rows_a)
    tensors = site_tensors.reshape(sec, phys, B, B).transpose(0, 2, 1, 3).reshape(rows_a, phys * B)
    target = route_owner[0, :, :, 0] * sec + route_sector[0]
    target = lax.dynamic_slice_in_dim(target, member * sec, sec, 0)
    goals = jnp.broadcast_to(target.T[:, :, None], (phys, sec, dr)).reshape(cols // 128, 128)
    goals = jnp.pad(goals.astype(BF16), ((0, 16 - cols // 128), (0, 0)))
    message = jnp.concatenate([tensors, goals], axis=0)
    index = jnp.arange(B, dtype=jnp.int32)
    flags = index[None, :] < live_block_extent[:, None]
    live = (flags[:, :, None] & flags[:, None, :]).astype(F32)
    start = psi.astype(F32).reshape(sec, B, B) * live
    live = jnp.tile(live.reshape(rows_a, B), (1, 4))
    start = jnp.tile(start.reshape(rows_a, B), (1, 4))

    count_all = float(sec * n_sector * B * B)
    dma = pltpu.SemaphoreType.DMA
    ground, energy = pl.pallas_call(
        functools.partial(kernel, n_site, n_sector, sec, phys, bond, count_all),
        out_shape=(
            jax.ShapeDtypeStruct((rows_a, 128), F32),
            jax.ShapeDtypeStruct((8, 128), F32),
        ),
        in_specs=[pl.BlockSpec(memory_space=pltpu.VMEM)] * 6,
        out_specs=[pl.BlockSpec(memory_space=pltpu.VMEM)] * 2,
        scratch_shapes=[
            pltpu.VMEM((phys, wide, wide), BF16),
            pltpu.VMEM((n_site, rows_a + 16, 128), BF16),
            pltpu.VMEM((steps, n_sector * own, wide), BF16),
            pltpu.VMEM((steps, n_sector, own, wide), BF16),
            pltpu.VMEM((steps, rows_a, wide), BF16),
            pltpu.VMEM((rows_a, wide), BF16),
            pltpu.VMEM((rows_a, wide), BF16),
            pltpu.VMEM((phys, rows_a, wide), BF16),
            pltpu.VMEM((cols, wide), BF16),
            pltpu.VMEM((DAV_ITERS + 1, n_sector, 8, 128), F32),
            pltpu.VMEM((DAV_ITERS + 1, 8, 128), F32),
            pltpu.VMEM((wide, rows_a), BF16),
            pltpu.VMEM((rows_a, wide), F32),
            dma((n_site,)), dma((n_site,)),
            dma((steps, n_sector)), dma((steps, n_sector)),
            dma((steps, n_site)), dma((steps, n_site)),
            dma((DAV_ITERS + 1, n_sector)), dma((DAV_ITERS + 1, n_sector)),
        ],
        compiler_params=pltpu.CompilerParams(
            collective_id=0, has_side_effects=True, vmem_limit_bytes=50 * 1024 * 1024
        ),
    )(env, mpo_terms, message, start, live, right)
    return ground[:, :B].reshape(1, sec, B * B), energy[0, :1]


def solution(mesh):
    in_specs = (
        P("sector", None, None),
        P(),
        P("site", "sector", None, None),
        P("site", None, None, None),
        P("site", None, None),
        P("sector"),
        P("site", "sector", None),
        P("site", "sector", None, None),
    )
    out_specs = (P("site", "sector", None), P("site"))
    return jax.shard_map(local, mesh=mesh, in_specs=in_specs, out_specs=out_specs, check_vma=False)
```

time: 540 us -> 98.8 us (0.18)
  blocking collectives: 379 us -> 0 us
  Pallas kernels: 0 us -> 86.8 us
  local copies, waits for them, and re-layouts: 75.3 us -> 9.88 us
  matrix products: 52.7 us -> 0 us
  between operations: 10 us -> 0.85 us
  starting transfers between devices: 8.46 us -> 0 us
    all_to_all x3 -> x0, blocking collectives: 191 us -> none  [route(): lax.all_to_all(outbox, 'sector', split_axis=0, concat_axis=0, tiled=True)]
    psum x10 -> x0, blocking collectives: 188 us -> none  [the longest x3 53.3 us: rayleigh(): return lax.psum(local_sum(trial_vector, image), 'sector') / count_all]
    pallas_call x0 -> x1, Pallas kernels: none -> 86.8 us  [local(): pl.pallas_call(functools.partial(kernel, n_site, n_sector, sec, phys, bon...]
    dot_general x19 -> x0, matrix products: 52.7 us -> none  [the longest x3 19.5 us: contract(): jnp.einsum('spad,spvac->spvdc', tensor_blocks, halfway, preferred_element...]
    convert_element_type x6 -> x2, local copies, waits for them, and re-layouts: 28.1 us -> 0.16 us  [the longest x1 0.1 us: local(): goals = jnp.pad(goals.astype(BF16), ((0, 16 - cols // 128), (0, 0)))]
    reshape x8 -> x12, local copies, waits for them, and re-layouts: 25.5 us -> 8.74 us  [the longest x3 3.53 us: local(): right_env.reshape(sec, bond, B, B).transpose(1, 2, 0, 3)]
    ppermute x3 -> x0, starting transfers between devices: 8.46 us -> none  [from_behind(): return lax.ppermute(block, axis, route)]
    another operation x3 -> x4, local copies, waits for them, and re-layouts: 6.36 us -> 0.22 us  [the longest x2 0.11 us: local(): start = jnp.tile(start.reshape(rows_a, B), (1, 4))]
  transfers between devices with their start and end apart: 3 -> 0, of which waited for: 3 -> 0; matrix products, arithmetic and copies ran while one was open for 0% -> 0% of each run, Pallas kernels for 0% -> 0%
where the time goes in v1:
time: 98.8 us; the launch traced here: 98.5 us
  Pallas kernels  86.8 us (88%)
  local copies, waits for them, and re-layouts  9.88 us (10%)
  other arithmetic  1.07 us (1%)
    pallas_call x1, Pallas kernels, local(): pl.pallas_call(functools.partial(kernel, n_site, n_sector, sec, phys, bon...  86.8 us
    reshape x3, local copies, waits for them, and re-layouts, local(): right_env.reshape(sec, bond, B, B).transpose(1, 2, 0, 3)  3.53 us
    reshape x4, local copies, waits for them, and re-layouts, local(): env_in.reshape(sec, bond, B, B).transpose(0, 2, 1, 3).reshape(rows_a, wide)  3.04 us

profile of v1, /device:TPU:0, one launch (start us, length us, event | category | flops | bytes accessed | tf_op | source)
XLA Modules:
  0.0 98.5 jit_solution(11367949032420860475)
XLA Ops:
  0.6 0.0 copy-start.3
  0.6 0.0 copy-start.2
  0.7 0.7 bitcast_add_fusion
  1.4 0.1 fusion.4
  1.4 0.1 broadcast_in_dim.2
  1.5 0.1 convert_element_type.22
  1.6 1.0 %reshape.110 = bf16[8,4,32,32]{3,2,1,0:T(8,128)(2,1)S(1)} reshape(bf16[1,8,4,1024]{3,2,1,0:T(4,128)(2,1)} %param.10) | data formatting | bytes 131072 | tf_op jit(solution)/shard_map/reshape | solution.py:316
  2.7 0.0 copy-start
  2.7 0.1 copy.28
  2.8 0.2 reshape.111
  3.0 0.0 copy-done.3
  3.0 0.1 iota_compare_fusion.1
  3.1 0.1 lt.31
  3.2 0.0 copy-done.2
  3.2 0.1 reshape.118
  3.3 0.1 fusion.2
  3.4 0.1 copy.18
  3.5 0.1 copy.23.start_ref
  3.6 0.1 fusion.1
  3.7 0.1 copy.19
  3.8 0.1 copy.24.mask_ref
  3.9 0.0 copy-done
  3.9 1.0 %reshape.108 = bf16[8,20,32,32]{3,2,0,1:T(8,128)(2,1)S(1)} reshape(bf16[8,20,1024]{2,0,1:T(8,128)(2,1)S(1)} %copy-done) | data formatting | bytes 655360 | tf_op jit(solution)/shard_map/reshape | solution.py:314
  4.9 0.9 copy.15
  5.8 0.9 reshape.109
  6.8 0.2 copy.21.env_ref
  7.0 2.0 %reshape.114 = bf16[8,20,32,32]{3,2,0,1:T(8,128)(2,1)S(1)} reshape(bf16[1,8,20,1024]{3,1,2,0:T(8,128)(2,1)} %param.15) | data formatting | bytes 655360 | tf_op jit(solution)/shard_map/reshape | solution.py:315
  9.0 0.6 copy.27
  9.6 0.0 copy-start.1
  9.6 0.9 reshape.115.right_ref
  10.5 0.0 copy-done.1
  10.5 86.8 %shard_map.95 = (f32[256,128]{1,0:T(8,128)S(1)}, f32[8,128]{1,0:T(8,128)S(1)}) custom-call(bf16[256,640]{1,0:T(8,128)(2,1)S(1)} %copy.21.env_ref, bf16[4,20,20]{2,1,0:T(8,128)(2,1)S(1)} %copy.22.mpo_ref, bf16[272,128]{1,0:T(8,128)(2,1)S(1)} %fusion.3.msg_ref, f32[256,128]{1,0:T(8,128)S(1)} %copy.23.start_ref, f32[256,128]{1,0:T(8,128)S(1)} %copy.24.mask_ref, ...), custom_call_target="tpu_custom_call" | custom-call | tf_op jit(solution)/shard_map/pallas_call | solution.py:331
  97.3 0.7 reshape.116
  98.0 0.5 slice.7
  (4 shorter events, 0.1 us)
Async XLA Ops:
  0.6 2.4 %copy-start.3 = (s32[8]{0:T(128)S(1)}, s32[8]{0:T(128)}, u32[]{:S(2)}) copy-start(s32[8]{0:T(128)} %param.13) | copy-start | bytes 100
  0.6 2.5 %copy-start.2 = (bf16[1,8,1024]{2,1,0:T(8,128)(2,1)S(1)}, bf16[1,8,1024]{2,1,0:T(8,128)(2,1)}, u32[]{:S(2)}) copy-start(bf16[1,8,1024]{2,1,0:T(8,128)(2,1)} %param.14) | copy-start | bytes 49156
  2.7 1.2 %copy-start = (bf16[8,20,1024]{2,0,1:T(8,128)(2,1)S(1)}, bf16[8,20,1024]{2,0,1:T(8,128)(2,1)}, u32[]{:S(2)}) copy-start(bf16[8,20,1024]{2,0,1:T(8,128)(2,1)} %param.8) | copy-start | bytes 983044
  9.6 0.9 copy-start.1

commit v2 on v1

v2 whole, which is shorter than its diff:
```python
import functools

import jax
import jax.numpy as jnp
from jax import lax
from jax.experimental import pallas as pl
from jax.experimental.pallas import tpu as pltpu
from jax.sharding import PartitionSpec as P

B = 32
DAV_ITERS = 2
MESH = pl.DeviceIdType.MESH
F32 = jnp.float32
BF16 = jnp.bfloat16

epsilon = 1e-06


def iota(shape, axis):
    return lax.broadcasted_iota(jnp.int32, shape, axis)


def flag(condition, kind=BF16):
    return jnp.where(condition, 1.0, 0.0).astype(F32).astype(kind)


def dot(left, right):
    return jnp.dot(left, right, preferred_element_type=F32)


def dot_rows(left, right):
    return lax.dot_general(left, right, (((1,), (1,)), ((), ())), preferred_element_type=F32)


def kernel(
    n_site, n_sector, sec, phys, bond, count_all, parts,
    env_ref, right_ref, tensor_ref, psi_ref, mpo_ref, goals_ref, extent_ref,
    ground_ref, energy_ref,
    mix, tbuf, part, xbuf, sbuf, rsbuf, ebuf, ecur, lbuf, zbuf, blocks, wbuf, leftbuf, routing,
    redbuf, redout, right_t, diag_right, qbuf, stage,
    t_send, t_recv, x_send, x_recv, rs_send, rs_recv, ag_send, ag_recv, red_send, red_recv,
):
    site = lax.axis_index("site")
    member = lax.axis_index("sector")
    n_low = 2
    n_high = n_sector // n_low
    high = member // n_low
    low = member % n_low
    rows_a = sec * B
    wide = bond * B
    chunks = wide // 128
    dr = B // n_site
    own = sec * dr
    cols = phys * own
    last = n_site - 1
    group = iota((B, 128), 0) & 3
    in_group = iota((B, 128), 1) >> 5 == group
    upper = iota((8, 128), 0) < 4
    takes = [[((group + turn) & 3 == k) & in_group for k in range(4)] for turn in range(4)]

    def unpack(rows):
        spread = [
            jnp.concatenate(
                [
                    jnp.where(
                        upper,
                        jnp.broadcast_to(stage[pl.ds(r, 1), pl.ds(256 * q, 128)], (8, 128)),
                        jnp.broadcast_to(stage[pl.ds(r, 1), pl.ds(256 * q + 128, 128)], (8, 128)),
                    )
                    for q in range(4)
                ],
                axis=0,
            )
            for r in rows
        ]
        whole = None
        for turn in range(4):
            moved = jnp.where(takes[turn][0], spread[0], 0.0)
            for k in range(1, 4):
                moved = jnp.where(takes[turn][k], spread[k], moved)
            whole = moved if turn == 0 else whole + pltpu.roll(moved, 32 * turn, 1)
        return whole

    def unpack_bonds(source, target):
        def one(s, carry):
            stage[pl.ds(0, bond)] = source[s].astype(F32)
            rows = pl.ds(pl.multiple_of(s * B, B), B)
            for j in range(chunks):
                target[rows, pl.ds(j * 128, 128)] = unpack(range(4 * j, 4 * j + 4)).astype(target.dtype)
            return carry

        lax.fori_loop(0, sec, one, 0)

    def site_peer(k):
        return lax.rem(site + k, n_site)

    def sector_peer(k):
        return lax.rem(member + k, n_sector)

    def high_peer(k):
        return lax.rem(high + k, n_high)

    barrier = pltpu.get_barrier_semaphore()
    for k in range(1, n_site):
        pl.semaphore_signal(barrier, inc=1, device_id=(site_peer(k), member), device_id_type=MESH)
    for k in range(1, n_sector):
        pl.semaphore_signal(barrier, inc=1, device_id=(site, sector_peer(k)), device_id_type=MESH)
    for s in range(sec):
        stage[pl.ds(0, phys)] = tensor_ref[s].astype(F32)
        tbuf[site, pl.ds(s * B, B)] = unpack(range(phys)).astype(BF16)
    tbuf[site, pl.ds(rows_a, 16)] = goals_ref[...]
    pl.semaphore_wait(barrier, n_site + n_sector - 2)

    def t_copy(k, source):
        return pltpu.make_async_remote_copy(
            src_ref=tbuf.at[source], dst_ref=tbuf.at[source],
            send_sem=t_send.at[k], recv_sem=t_recv.at[source],
            device_id=(site_peer(k), member), device_id_type=MESH,
        )

    def t_start():
        for k in range(1, n_site):
            t_copy(k, site).start()

    pl.when(site == 0)(t_start)

    spread_rows = flag(iota((wide, bond), 0) >> 5 == iota((wide, bond), 1))
    spread_cols = flag(iota((bond, wide), 1) >> 5 == iota((bond, wide), 0))
    eye_wide = flag((iota((wide, wide), 0) - iota((wide, wide), 1)) & 31 == 0)
    for p in range(phys):
        tall = dot(spread_rows, mpo_ref[p]).astype(BF16)
        mix[p] = dot(tall, spread_cols).astype(BF16) * eye_wide

    row, col = iota((rows_a, rows_a), 0), iota((rows_a, rows_a), 1)
    permute = flag(col == (row % B) // dr * own + row // B * dr + row % dr)
    row, col = iota((cols, phys * B), 0), iota((cols, phys * B), 1)
    pick_rows = flag((row // own == col // B) & (col % B == site * dr + row % dr))
    row, col = iota((cols, rows_a), 0), iota((cols, rows_a), 1)
    same_sector = flag((row % own) // dr == col // B)
    row, col = iota((phys * B, phys * 128), 0), iota((phys * B, phys * 128), 1)
    repeat4 = flag((row >> 5 == col >> 7) & (row & 31 == col & 31))
    row, col = iota((128, phys * 128), 0), iota((128, phys * 128), 1)
    block4 = flag(row >> 5 == (col & 127) >> 5)

    @pl.when((site > 0) & (site < last))
    def _():
        t_start()

    def prepare(step):
        @pl.when(step != site)
        def _():
            t_copy(1, step).wait_recv()

        tensors = tbuf[step, pl.ds(0, rows_a)]
        goals = tbuf[step, pl.ds(rows_a, 16)].astype(F32)
        repeated = dot(tensors, repeat4).astype(BF16)
        for s in range(sec):
            piece = repeated[s * B:(s + 1) * B]
            wbuf[s] = jnp.concatenate([piece] * 4, axis=0) * block4
        leftbuf[...] = dot_rows(pick_rows, tensors).astype(BF16) * same_sector
        goal_row = jnp.concatenate([goals[r:r + 1] for r in range(cols // 128)], axis=1)
        rows_all = n_sector * own
        row, col = iota((rows_all, cols), 0), iota((rows_all, cols), 1)
        wanted = jnp.where((row - col) & (dr - 1) == 0, (row // dr).astype(F32), -1.0)
        routing[...] = flag(wanted == goal_row)

    def prepare_right():
        unpack_bonds(right_ref, qbuf)
        right_t[...] = qbuf[...].T.astype(BF16)

    def right_diagonal():
        row, col = iota((wide, rows_a), 0), iota((wide, rows_a), 1)
        masked = right_t[...] * flag((row - col) & 31 == 0)
        folded = dot(spread_cols, masked).astype(BF16)
        diag_right[...] = dot(spread_rows, folded).astype(BF16)

    unpack_bonds(env_ref, ecur)
    prepare(0)

    @pl.when(site == 0)
    def _():
        lbuf[...] = ecur[...]

    def chunk_rows(high_of, low_of):
        return pl.ds(pl.multiple_of((high_of * n_low + low_of) * own, own), own)

    def x_copy(step, c, k):
        lanes = pl.ds(*parts[c])
        block = high_peer(k)
        return pltpu.make_async_remote_copy(
            src_ref=part.at[step, chunk_rows(block, 1 - low), lanes],
            dst_ref=xbuf.at[step, k, :, lanes],
            send_sem=x_send.at[step, c, k], recv_sem=x_recv.at[step, c, k],
            device_id=(site, high * n_low + 1 - low), device_id_type=MESH,
        )

    def rs_copy(step, c, k, source):
        lanes = pl.ds(*parts[c])
        return pltpu.make_async_remote_copy(
            src_ref=sbuf.at[step, k, :, lanes],
            dst_ref=rsbuf.at[step, source, :, lanes],
            send_sem=rs_send.at[step, c, k], recv_sem=rs_recv.at[step, c, source],
            device_id=(site, high_peer(k) * n_low + low), device_id_type=MESH,
        )

    def ag_copy(step, c, k, source):
        lanes = pl.ds(*parts[c])
        rows = pl.ds(pl.multiple_of(source * own, own), own)
        return pltpu.make_async_remote_copy(
            src_ref=ebuf.at[step, rows, lanes], dst_ref=ebuf.at[step, rows, lanes],
            send_sem=ag_send.at[step, c, k], recv_sem=ag_recv.at[step, c, source],
            device_id=(site_peer(k), member), device_id_type=MESH,
        )

    n_parts = len(parts)
    order = list(range(1, n_high)) + [0]

    def chain_step(step, carry):
        for s in range(sec):
            rows = pl.ds(s * B, B)
            stacked = jnp.concatenate([ecur[rows, pl.ds(j * 128, 128)] for j in range(chunks)], axis=0)
            product = dot(stacked, wbuf[s]).astype(BF16)
            for p in range(phys):
                for j in range(chunks):
                    zbuf[p, rows, pl.ds(j * 128, 128)] = product[j * B:(j + 1) * B, p * 128:(p + 1) * 128]
        for p in range(phys):
            half = dot(leftbuf[pl.ds(p * own, own)], zbuf[p]).astype(BF16)
            blocks[pl.ds(p * own, own)] = dot(half, mix[p]).astype(BF16)
        for k in order:
            rows = pl.ds(pl.multiple_of(high_peer(k) * n_low * own, n_low * own), n_low * own)
            part[step, rows] = dot(routing[rows], blocks[...]).astype(BF16)
            x_copy(step, 0, k).start()
        for c in range(1, n_parts):
            for k in order:
                x_copy(step, c, k).start()

        @pl.when(step + 1 < last)
        def _():
            prepare(step + 1)

        pl.when(step == 0)(prepare_right)
        pl.when(step + 1 == last)(right_diagonal)

        totals = []
        for c in range(n_parts):
            lanes = pl.ds(*parts[c])
            for k in order:
                x_copy(step, c, k).wait_recv()
                mine = part[step, chunk_rows(high_peer(k), low), lanes].astype(F32)
                mine = mine + xbuf[step, k, :, lanes].astype(F32)
                if k == 0:
                    totals.append(mine)
                else:
                    sbuf[step, k, :, lanes] = mine.astype(BF16)
                    rs_copy(step, c, k, high).start()
        for c in range(n_parts):
            lanes = pl.ds(*parts[c])
            total = totals[c]
            for k in range(1, n_high):
                source = high_peer(k)
                rs_copy(step, c, k, source).wait_recv()
                total = total + rsbuf[step, source, :, lanes].astype(F32)
            ebuf[step, pl.ds(pl.multiple_of(site * own, own), own), lanes] = total.astype(BF16)
            for k in range(1, n_site):
                @pl.when((step < last - 1) | (site_peer(k) == last))
                def _():
                    ag_copy(step, c, k, site).start()

        @pl.when((step < last - 1) | (site == last))
        def _():
            for c in range(n_parts):
                lanes = pl.ds(*parts[c])
                for k in range(1, n_site):
                    ag_copy(step, c, k, site_peer(k)).wait_recv()
                ecur[:, lanes] = dot(permute, ebuf[step, :, lanes]).astype(BF16)

        @pl.when(step + 1 == site)
        def _():
            lbuf[...] = ecur[...]

        return carry

    lax.fori_loop(0, last, chain_step, 0)

    row, col = iota((rows_a, 128), 0), iota((rows_a, 128), 1)
    extent = extent_ref[...]
    live = flag(((row & 31).astype(F32) < extent) & ((col & 31).astype(F32) < extent), F32)
    row, col = iota((rows_a, rows_a), 0), iota((rows_a, rows_a), 1)
    own_lanes = flag(row >> 5 == col >> 5, F32)
    row, col = iota((128, 128), 0), iota((128, 128), 1)
    same4 = flag(row >> 5 == col >> 5)
    row, col = iota((rows_a, wide), 0), iota((rows_a, wide), 1)
    left_diag = lbuf[...] * flag((row - col) & 31 == 0)

    def four_copies(values):
        values = values + pltpu.roll(values, 32, 1)
        return values + pltpu.roll(values, 64, 1)

    def own_sector(values):
        values = values * own_lanes
        folded = values[:, 0:128]
        for j in range(1, rows_a // 128):
            folded = folded + values[:, j * 128:(j + 1) * 128]
        return four_copies(folded)

    def operate(x):
        x = x.astype(BF16)
        for s in range(sec):
            rows = pl.ds(s * B, B)
            weights = jnp.concatenate([x[s * B:(s + 1) * B]] * 4, axis=0) * same4
            stacked = jnp.concatenate([lbuf[rows, pl.ds(j * 128, 128)] for j in range(chunks)], axis=0)
            product = dot(stacked, weights).astype(BF16)
            for j in range(chunks):
                ecur[rows, pl.ds(j * 128, 128)] = product[j * B:(j + 1) * B]
        return own_sector(dot(ecur[...], right_t[...])) * live

    def red_copy(turn, k, source):
        return pltpu.make_async_remote_copy(
            src_ref=redout.at[turn], dst_ref=redbuf.at[turn, source],
            send_sem=red_send.at[turn, k], recv_sem=red_recv.at[turn, source],
            device_id=(site, sector_peer(k)), device_id_type=MESH,
        )

    def reduce(turn, pairs, meanwhile=None):
        sums = [jnp.sum(x * y, axis=0, keepdims=True) for x, y in pairs]
        sums = sums + [jnp.zeros((1, 128), F32)] * (8 - len(sums))
        redout[turn] = jnp.concatenate(sums, axis=0)
        for k in range(1, n_sector):
            red_copy(turn, k, member).start()
        redbuf[turn, member] = redout[turn]
        made = meanwhile() if meanwhile else None
        for k in range(1, n_sector):
            red_copy(turn, k, sector_peer(k)).wait_recv()
        total = redbuf[turn, 0]
        for j in range(1, n_sector):
            total = total + redbuf[turn, j]
        total = jnp.sum(total, axis=1, keepdims=True) * (0.25 / count_all)
        return [total[j:j + 1] for j in range(len(pairs))], made

    stage[pl.ds(0, sec)] = psi_ref[...].astype(F32)
    start = jnp.concatenate([unpack([s] * 4) for s in range(sec)], axis=0) * live
    image = operate(start)
    (norm, energy), precond = reduce(
        0, [(start, start), (start, image)], lambda: own_sector(dot(left_diag, diag_right[...]))
    )
    scale = 1.0 / jnp.sqrt(norm + epsilon)
    vector = start * scale
    image = image * scale
    energy = energy * scale * scale
    for turn in range(1, DAV_ITERS + 1):
        correction = (image - energy * vector) / jnp.maximum(precond - energy, 1.0)
        applied = operate(correction)
        (vc, cc, vv, ci, ca, va, vi), _ = reduce(
            turn,
            [
                (vector, correction), (correction, correction), (vector, vector), (correction, image),
                (correction, applied), (vector, applied), (vector, image),
            ],
        )
        length_sq = jnp.maximum(cc - 2.0 * vc * vc + vc * vc * vv, 0.0)
        scale = 1.0 / jnp.sqrt(length_sq + epsilon)
        direction = (correction - vc * vector) * scale
        applied = (applied - vc * image) * scale
        coupling = (ci - vc * vi) * scale
        curvature = (ca - vc * ci - vc * va + vc * vc * vi) * scale * scale
        crossing = (va - vc * vi) * scale
        y, x = -2.0 * coupling, curvature - energy
        largest = jnp.maximum(jnp.abs(x), jnp.abs(y))
        safe = jnp.where(largest > 0.0, largest, 1.0)
        x, y = jnp.where(largest > 0.0, x / safe, 1.0), y / safe
        radius = jnp.sqrt(x * x + y * y)
        big = jnp.sqrt((radius + jnp.abs(x)) / (2.0 * radius))
        small = jnp.abs(y) / (2.0 * radius * big)
        cosine = jnp.where(x >= 0.0, big, small)
        sine = jnp.where(x >= 0.0, small, big) * jnp.where(y > 0.0, 1.0, -1.0)
        energy = cosine * cosine * vi + cosine * sine * (crossing + coupling) + sine * sine * curvature
        vector = cosine * vector + sine * direction
        image = cosine * image + sine * applied
    row, col = iota((rows_a, 128), 0), iota((rows_a, 128), 1)
    for j in range(B * B // 128):
        kept = jnp.where((row & 31) == (col >> 5) + 4 * j, vector, 0.0)
        ground_ref[:, pl.ds(j * 128, 128)] = jnp.sum(kept.reshape(sec, B, 128), axis=1)
    energy_ref[...] = jnp.broadcast_to(energy, (8, 128))

    @pl.when(site < last)
    def _():
        for k in range(1, n_site):
            t_copy(k, site).wait_send()

    def sent(step, carry):
        for c in range(n_parts):
            for k in range(n_high):
                x_copy(step, c, k).wait_send()
                if k > 0:
                    rs_copy(step, c, k, high).wait_send()
            for k in range(1, n_site):
                @pl.when((step < last - 1) | (site_peer(k) == last))
                def _():
                    ag_copy(step, c, k, site).wait_send()
        return carry

    lax.fori_loop(0, last, sent, 0)
    for turn in range(DAV_ITERS + 1):
        for k in range(1, n_sector):
            red_copy(turn, k, member).wait_send()


def local(
    env_in, mpo_terms, site_tensors, route_owner, route_sector, live_block_extent, psi, right_env
):
    n_sector = lax.axis_size("sector")
    n_site = lax.axis_size("site")
    member = lax.axis_index("sector")
    sec, bond = env_in.shape[0], env_in.shape[1]
    phys = site_tensors.shape[2]
    steps = n_site - 1
    n_high = n_sector // 2
    dr = B // n_site
    own = sec * dr
    cols = phys * own
    rows_a, wide = sec * B, bond * B
    cut = (wide // 128 + 1) // 2 * 128
    parts = ((0, cut), (cut, wide - cut))

    target = route_owner[0, :, :, 0] * sec + route_sector[0]
    target = lax.dynamic_slice_in_dim(target, member * sec, sec, 0)
    goals = jnp.broadcast_to(target.T[:, :, None], (phys, sec, dr)).reshape(cols // 128, 128)
    goals = jnp.pad(goals.astype(BF16), ((0, 16 - cols // 128), (0, 0)))
    extent = jnp.broadcast_to(live_block_extent.astype(F32)[:, None, None], (sec, B, 128)).reshape(rows_a, 128)

    count_all = float(sec * n_sector * B * B)
    dma = pltpu.SemaphoreType.DMA
    ground, energy = pl.pallas_call(
        functools.partial(kernel, n_site, n_sector, sec, phys, bond, count_all, parts),
        out_shape=(
            jax.ShapeDtypeStruct((sec, B * B), F32),
            jax.ShapeDtypeStruct((8, 128), F32),
        ),
        in_specs=[pl.BlockSpec(memory_space=pltpu.VMEM)] * 7,
        out_specs=[pl.BlockSpec(memory_space=pltpu.VMEM)] * 2,
        scratch_shapes=[
            pltpu.VMEM((phys, wide, wide), BF16),
            pltpu.VMEM((n_site, rows_a + 16, 128), BF16),
            pltpu.VMEM((steps, n_sector * own, wide), BF16),
            pltpu.VMEM((steps, n_high, own, wide), BF16),
            pltpu.VMEM((steps, n_high, own, wide), BF16),
            pltpu.VMEM((steps, n_high, own, wide), BF16),
            pltpu.VMEM((steps, rows_a, wide), BF16),
            pltpu.VMEM((rows_a, wide), BF16),
            pltpu.VMEM((rows_a, wide), BF16),
            pltpu.VMEM((phys, rows_a, wide), BF16),
            pltpu.VMEM((cols, wide), BF16),
            pltpu.VMEM((sec, 128, phys * 128), BF16),
            pltpu.VMEM((cols, rows_a), BF16),
            pltpu.VMEM((n_sector * own, cols), BF16),
            pltpu.VMEM((DAV_ITERS + 1, n_sector, 8, 128), F32),
            pltpu.VMEM((DAV_ITERS + 1, 8, 128), F32),
            pltpu.VMEM((wide, rows_a), BF16),
            pltpu.VMEM((wide, rows_a), BF16),
            pltpu.VMEM((rows_a, wide), F32),
            pltpu.VMEM((max(bond, sec) + 4, B * B), F32),
            dma((n_site,)), dma((n_site,)),
            dma((steps, 2, n_high)), dma((steps, 2, n_high)),
            dma((steps, 2, n_high)), dma((steps, 2, n_high)),
            dma((steps, 2, n_site)), dma((steps, 2, n_site)),
            dma((DAV_ITERS + 1, n_sector)), dma((DAV_ITERS + 1, n_sector)),
        ],
        compiler_params=pltpu.CompilerParams(
            collective_id=0, has_side_effects=True, vmem_limit_bytes=50 * 1024 * 1024
        ),
    )(env_in, right_env[0], site_tensors[0], psi[0], mpo_terms, goals, extent)
    return ground[None], energy[0, :1]


def solution(mesh):
    in_specs = (
        P("sector", None, None),
        P(),
        P("site", "sector", None, None),
        P("site", None, None, None),
        P("site", None, None),
        P("sector"),
        P("site", "sector", None),
        P("site", "sector", None, None),
    )
    out_specs = (P("site", "sector", None), P("site"))
    return jax.shard_map(local, mesh=mesh, in_specs=in_specs, out_specs=out_specs, check_vma=False)
```

time: 98.8 us -> 80.1 us (0.81)
  Pallas kernels: 86.8 us -> 74.4 us
  local copies, waits for them, and re-layouts: 9.88 us -> 4.57 us
  other arithmetic: 1.07 us -> 0.08 us
    pallas_call x1, Pallas kernels: 86.8 us -> 74.4 us  [local(): pl.pallas_call(functools.partial(kernel, n_site, n_sector, sec, phys, bon...]
    reshape x12 -> x0, local copies, waits for them, and re-layouts: 8.74 us -> none  [the longest x3 3.53 us: local(): right_env.reshape(sec, bond, B, B).transpose(1, 2, 0, 3)]
    unnamed x9 -> x18, local copies, waits for them, and re-layouts: 0.03 us -> 3.65 us
where the time goes in v2:
time: 80.1 us; the launch traced here: 79.8 us
  Pallas kernels  74.4 us (93%)
  local copies, waits for them, and re-layouts  4.57 us (6%)
    pallas_call x1, Pallas kernels, local(): pl.pallas_call(functools.partial(kernel, n_site, n_sector, sec, phys, bon...  74.4 us
    unnamed x18, local copies, waits for them, and re-layouts  3.65 us

profile of v2, /device:TPU:0, one launch (start us, length us, event | category | flops | bytes accessed | tf_op | source)
XLA Modules:
  0.0 79.8 jit_solution(15094626424998258505)
XLA Ops:
  0.6 0.0 copy-start.6
  0.6 0.0 copy-start.5
  0.7 0.0 copy-start.4
  0.7 0.6 copy-done.6
  1.3 0.0 copy-done.5
  1.3 0.0 copy-done.4
  1.3 0.0 copy-start.3
  1.4 0.1 fusion
  1.4 0.1 broadcast_in_dim.20
  1.5 0.1 broadcast_in_dim.21
  1.6 0.1 broadcast_in_dim.19
  1.7 0.1 convert_element_type.17
  1.8 0.3 copy-done.3
  2.1 0.1 broadcast_in_dim.22.extent_ref
  2.2 0.0 copy-start.2
  2.2 1.2 %copy.12.env_ref = bf16[8,20,1024]{2,1,0:T(8,128)(2,1)S(1)} copy(bf16[8,20,1024]{2,0,1:T(8,128)(2,1)} %param.8) | data formatting | bytes 655360 | tf_op args[0]
  3.4 0.0 copy-done.2
  3.4 0.0 copy-start
  3.4 0.0 copy-start.1
  3.4 0.2 copy.15
  3.6 0.6 copy-done
  4.3 0.0 copy-done.1
  4.3 74.4 %shard_map.95 = (f32[8,1024]{1,0:T(8,128)S(1)}, f32[8,128]{1,0:T(8,128)S(1)}) custom-call(bf16[8,20,1024]{2,1,0:T(8,128)(2,1)S(1)} %copy.12.env_ref, bf16[8,20,1024]{2,1,0:T(8,128)(2,1)S(1)} %bitcast.14, bf16[8,4,1024]{2,1,0:T(4,128)(2,1)S(1)} %bitcast.15, bf16[8,1024]{1,0:T(8,128)(2,1)S(1)} %bitcast.17, bf16[4,20,20]{2,1,0:T(8,128)(2,1)S(1)} %copy.13.mpo_ref, ...), custom_call_target="tpu_custom_call" | custom-call | tf_op jit(solution)/shard_map/pallas_call | solution.py:433
  78.7 0.5 slice.3
  79.2 0.6 copy.17
  (4 shorter events, 0.0 us)
Async XLA Ops:
  0.6 0.7 copy-start.6
  0.6 0.7 copy-start.5
  0.7 0.7 copy-start.4
  1.3 0.7 copy-start.3
  2.2 1.2 %copy-start.2 = (bf16[1,8,20,1024]{3,1,2,0:T(8,128)(2,1)S(1)}, bf16[1,8,20,1024]{3,1,2,0:T(8,128)(2,1)}, u32[]{:S(2)}) copy-start(bf16[1,8,20,1024]{3,1,2,0:T(8,128)(2,1)} %param.15) | copy-start | bytes 983044
  3.4 0.8 %copy-start = (bf16[1,8,4,1024]{3,2,1,0:T(4,128)(2,1)S(1)}, bf16[1,8,4,1024]{3,2,1,0:T(4,128)(2,1)}, u32[]{:S(2)}) copy-start(bf16[1,8,4,1024]{3,2,1,0:T(4,128)(2,1)} %param.10) | copy-start | bytes 196612
  3.4 0.8 %copy-start.1 = (bf16[1,8,1024]{2,1,0:T(8,128)(2,1)S(1)}, bf16[1,8,1024]{2,1,0:T(8,128)(2,1)}, u32[]{:S(2)}) copy-start(bf16[1,8,1024]{2,1,0:T(8,128)(2,1)} %param.14) | copy-start | bytes 49156

commit v3 on v2

--- a/solution.py
+++ b/solution.py
@@ -36,9 +36,9 @@
     n_site, n_sector, sec, phys, bond, count_all, parts,
     env_ref, right_ref, tensor_ref, psi_ref, mpo_ref, goals_ref, extent_ref,
     ground_ref, energy_ref,
-    mix, tbuf, part, xbuf, sbuf, rsbuf, ebuf, ecur, lbuf, zbuf, blocks, wbuf, leftbuf, routing,
-    redbuf, redout, right_t, diag_right, qbuf, stage,
-    t_send, t_recv, x_send, x_recv, rs_send, rs_recv, ag_send, ag_recv, red_send, red_recv,
+    mix, tbuf, part, xbuf, sbuf, rsbuf, ebuf, ecur, lbuf, zbuf, halves, wbuf, leftbuf, routing,
+    redbuf, redout, right_t, diag_right, qbuf, stage, env_in, right_in,
+    t_send, t_recv, x_send, x_recv, rs_send, rs_recv, ag_send, ag_recv, red_send, red_recv, fetch_sem,
 ):
     site = lax.axis_index("site")
     member = lax.axis_index("sector")
@@ -58,20 +58,20 @@
     upper = iota((8, 128), 0) < 4
     takes = [[((group + turn) & 3 == k) & in_group for k in range(4)] for turn in range(4)]
 
-    def unpack(rows):
+    def unpack(pieces):
         spread = [
             jnp.concatenate(
                 [
                     jnp.where(
                         upper,
-                        jnp.broadcast_to(stage[pl.ds(r, 1), pl.ds(256 * q, 128)], (8, 128)),
-                        jnp.broadcast_to(stage[pl.ds(r, 1), pl.ds(256 * q + 128, 128)], (8, 128)),
+                        jnp.broadcast_to(piece(pl.ds(256 * q, 128)), (8, 128)),
+                        jnp.broadcast_to(piece(pl.ds(256 * q + 128, 128)), (8, 128)),
                     )
                     for q in range(4)
                 ],
                 axis=0,
             )
-            for r in rows
+            for piece in pieces
         ]
         whole = None
         for turn in range(4):
@@ -82,14 +82,16 @@
         return whole
 
     def unpack_bonds(source, target):
-        def one(s, carry):
-            stage[pl.ds(0, bond)] = source[s].astype(F32)
-            rows = pl.ds(pl.multiple_of(s * B, B), B)
-            for j in range(chunks):
-                target[rows, pl.ds(j * 128, 128)] = unpack(range(4 * j, 4 * j + 4)).astype(target.dtype)
+        stage[...] = source[...].astype(F32)
+
+        def one(j, carry):
+            lanes_out = pl.ds(pl.multiple_of(j * 128, 128), 128)
+            for s in range(sec):
+                pieces = [lambda lanes, k=k: stage[4 * j + k, pl.ds(s, 1), lanes] for k in range(4)]
+                target[pl.ds(s * B, B), lanes_out] = unpack(pieces).astype(target.dtype)
             return carry
 
-        lax.fori_loop(0, sec, one, 0)
+        lax.fori_loop(0, chunks, one, 0)
 
     def site_peer(k):
         return lax.rem(site + k, n_site)
@@ -100,14 +102,23 @@
     def high_peer(k):
         return lax.rem(high + k, n_high)
 
+    def fetch_env():
+        return pltpu.make_async_copy(env_ref, env_in, fetch_sem.at[0])
+
+    def fetch_right():
+        return pltpu.make_async_copy(right_ref, right_in, fetch_sem.at[1])
+
+    fetch_env().start()
+    fetch_right().start()
     barrier = pltpu.get_barrier_semaphore()
     for k in range(1, n_site):
         pl.semaphore_signal(barrier, inc=1, device_id=(site_peer(k), member), device_id_type=MESH)
     for k in range(1, n_sector):
         pl.semaphore_signal(barrier, inc=1, device_id=(site, sector_peer(k)), device_id_type=MESH)
     for s in range(sec):
-        stage[pl.ds(0, phys)] = tensor_ref[s].astype(F32)
-        tbuf[site, pl.ds(s * B, B)] = unpack(range(phys)).astype(BF16)
+        stage[0, pl.ds(0, phys)] = tensor_ref[s].astype(F32)
+        pieces = [lambda lanes, p=p: stage[0, pl.ds(p, 1), lanes] for p in range(phys)]
+        tbuf[site, pl.ds(s * B, B)] = unpack(pieces).astype(BF16)
     tbuf[site, pl.ds(rows_a, 16)] = goals_ref[...]
     pl.semaphore_wait(barrier, n_site + n_sector - 2)
 
@@ -123,6 +134,7 @@
             t_copy(k, site).start()
 
     pl.when(site == 0)(t_start)
+
 
     spread_rows = flag(iota((wide, bond), 0) >> 5 == iota((wide, bond), 1))
     spread_cols = flag(iota((bond, wide), 1) >> 5 == iota((bond, wide), 0))
@@ -165,7 +177,8 @@
         routing[...] = flag(wanted == goal_row)
 
     def prepare_right():
-        unpack_bonds(right_ref, qbuf)
+        fetch_right().wait()
+        unpack_bonds(right_in, qbuf)
         right_t[...] = qbuf[...].T.astype(BF16)
 
     def right_diagonal():
@@ -174,7 +187,8 @@
         folded = dot(spread_cols, masked).astype(BF16)
         diag_right[...] = dot(spread_rows, folded).astype(BF16)
 
-    unpack_bonds(env_ref, ecur)
+    fetch_env().wait()
+    unpack_bonds(env_in, ecur)
     prepare(0)
 
     @pl.when(site == 0)
@@ -224,14 +238,15 @@
                 for j in range(chunks):
                     zbuf[p, rows, pl.ds(j * 128, 128)] = product[j * B:(j + 1) * B, p * 128:(p + 1) * 128]
         for p in range(phys):
-            half = dot(leftbuf[pl.ds(p * own, own)], zbuf[p]).astype(BF16)
-            blocks[pl.ds(p * own, own)] = dot(half, mix[p]).astype(BF16)
-        for k in order:
-            rows = pl.ds(pl.multiple_of(high_peer(k) * n_low * own, n_low * own), n_low * own)
-            part[step, rows] = dot(routing[rows], blocks[...]).astype(BF16)
-            x_copy(step, 0, k).start()
-        for c in range(1, n_parts):
+            halves[pl.ds(p * own, own)] = dot(leftbuf[pl.ds(p * own, own)], zbuf[p]).astype(BF16)
+        for c in range(n_parts):
+            lanes = pl.ds(*parts[c])
+            made = jnp.concatenate(
+                [dot(halves[pl.ds(p * own, own)], mix[p, :, lanes]).astype(BF16) for p in range(phys)], axis=0
+            )
             for k in order:
+                rows = pl.ds(pl.multiple_of(high_peer(k) * n_low * own, n_low * own), n_low * own)
+                part[step, rows, lanes] = dot(routing[rows], made).astype(BF16)
                 x_copy(step, c, k).start()
 
         @pl.when(step + 1 < last)
@@ -337,8 +352,10 @@
         total = jnp.sum(total, axis=1, keepdims=True) * (0.25 / count_all)
         return [total[j:j + 1] for j in range(len(pairs))], made
 
-    stage[pl.ds(0, sec)] = psi_ref[...].astype(F32)
-    start = jnp.concatenate([unpack([s] * 4) for s in range(sec)], axis=0) * live
+    stage[0] = psi_ref[...].astype(F32)
+    start = jnp.concatenate(
+        [unpack([lambda lanes, s=s: stage[0, pl.ds(s, 1), lanes]] * 4) for s in range(sec)], axis=0
+    ) * live
     image = operate(start)
     (norm, energy), precond = reduce(
         0, [(start, start), (start, image)], lambda: own_sector(dot(left_diag, diag_right[...]))
@@ -380,7 +397,7 @@
     for j in range(B * B // 128):
         kept = jnp.where((row & 31) == (col >> 5) + 4 * j, vector, 0.0)
         ground_ref[:, pl.ds(j * 128, 128)] = jnp.sum(kept.reshape(sec, B, 128), axis=1)
-    energy_ref[...] = jnp.broadcast_to(energy, (8, 128))
+    energy_ref[0] = energy[0, 0]
 
     @pl.when(site < last)
     def _():
@@ -419,8 +436,8 @@
     own = sec * dr
     cols = phys * own
     rows_a, wide = sec * B, bond * B
-    cut = (wide // 128 + 1) // 2 * 128
-    parts = ((0, cut), (cut, wide - cut))
+    parts = tuple((at, min(256, wide - at)) for at in range(0, wide, 256))
+    n_parts = len(parts)
 
     target = route_owner[0, :, :, 0] * sec + route_sector[0]
     target = lax.dynamic_slice_in_dim(target, member * sec, sec, 0)
@@ -434,10 +451,10 @@
         functools.partial(kernel, n_site, n_sector, sec, phys, bond, count_all, parts),
         out_shape=(
             jax.ShapeDtypeStruct((sec, B * B), F32),
-            jax.ShapeDtypeStruct((8, 128), F32),
+            jax.ShapeDtypeStruct((1,), F32),
         ),
-        in_specs=[pl.BlockSpec(memory_space=pltpu.VMEM)] * 7,
-        out_specs=[pl.BlockSpec(memory_space=pltpu.VMEM)] * 2,
+        in_specs=[pl.BlockSpec(memory_space=pltpu.HBM if i < 2 else pltpu.VMEM) for i in range(7)],
+        out_specs=[pl.BlockSpec(memory_space=pltpu.VMEM), pl.BlockSpec(memory_space=pltpu.SMEM)],
         scratch_shapes=[
             pltpu.VMEM((phys, wide, wide), BF16),
             pltpu.VMEM((n_site, rows_a + 16, 128), BF16),
@@ -458,18 +475,21 @@
             pltpu.VMEM((wide, rows_a), BF16),
             pltpu.VMEM((wide, rows_a), BF16),
             pltpu.VMEM((rows_a, wide), F32),
-            pltpu.VMEM((max(bond, sec) + 4, B * B), F32),
+            pltpu.VMEM((bond, sec, B * B), F32),
+            pltpu.VMEM((bond, sec, B * B), BF16),
+            pltpu.VMEM((bond, sec, B * B), BF16),
             dma((n_site,)), dma((n_site,)),
-            dma((steps, 2, n_high)), dma((steps, 2, n_high)),
-            dma((steps, 2, n_high)), dma((steps, 2, n_high)),
-            dma((steps, 2, n_site)), dma((steps, 2, n_site)),
+            dma((steps, n_parts, n_high)), dma((steps, n_parts, n_high)),
+            dma((steps, n_parts, n_high)), dma((steps, n_parts, n_high)),
+            dma((steps, n_parts, n_site)), dma((steps, n_parts, n_site)),
             dma((DAV_ITERS + 1, n_sector)), dma((DAV_ITERS + 1, n_sector)),
+            dma((2,)),
         ],
         compiler_params=pltpu.CompilerParams(
             collective_id=0, has_side_effects=True, vmem_limit_bytes=50 * 1024 * 1024
         ),
-    )(env_in, right_env[0], site_tensors[0], psi[0], mpo_terms, goals, extent)
-    return ground[None], energy[0, :1]
+    )(env_in.transpose(1, 0, 2), right_env[0].transpose(1, 0, 2), site_tensors[0], psi[0], mpo_terms, goals, extent)
+    return ground[None], energy
 
 
 def solution(mesh):

time: 80.1 us -> 82 us (1.024)
  between operations: 0.73 us -> 2.51 us
where the time goes in v3:
time: 82 us; the launch traced here: 81.6 us
  Pallas kernels  74.3 us (91%)
  local copies, waits for them, and re-layouts  4.71 us (6%)
  between operations  2.51 us (3%)
    pallas_call x1, Pallas kernels, local(): pl.pallas_call(functools.partial(kernel, n_site, n_sector, sec, phys, bon...  74.3 us
    unnamed x18, local copies, waits for them, and re-layouts  4.3 us

profile of v3, /device:TPU:0, one launch (start us, length us, event | category | flops | bytes accessed | tf_op | source)
XLA Modules:
  0.0 81.6 jit_solution(7450433552179637400)
XLA Ops:
  0.6 0.0 copy-start.7
  0.6 0.0 copy-start.6
  0.7 0.0 copy-start.5
  0.7 0.6 copy-done.7
  1.3 0.0 copy-done.6
  1.3 0.0 copy-done.5
  1.3 0.0 copy-start.4
  1.4 0.1 fusion
  1.4 0.1 broadcast_in_dim.20
  1.5 0.1 broadcast_in_dim.21
  1.6 0.1 broadcast_in_dim.19
  1.7 0.1 convert_element_type.17
  1.8 0.3 copy-done.4
  2.1 0.0 copy-start.2
  2.1 0.0 copy-start.3
  2.1 0.1 broadcast_in_dim.22.extent_ref
  2.2 0.7 copy-done.2
  2.9 0.0 copy-done.3
  2.9 0.0 copy-start
  2.9 1.0 %copy-done = bf16[8,20,1024]{2,0,1:T(8,128)(2,1)S(1)} copy-done((bf16[8,20,1024]{2,0,1:T(8,128)(2,1)S(1)}, bf16[8,20,1024]{2,0,1:T(8,128)(2,1)}, u32[]{:S(2)}) %copy-start) | copy-done | bytes 327704
  3.9 0.0 copy-start.1
  3.9 1.0 %copy-done.1 = bf16[1,8,20,1024]{3,1,2,0:T(8,128)(2,1)S(1)} copy-done((bf16[1,8,20,1024]{3,1,2,0:T(8,128)(2,1)S(1)}, bf16[1,8,20,1024]{3,1,2,0:T(8,128)(2,1)}, u32[]{:S(2)}) %copy-start.1) | copy-done | bytes 327704
  4.9 74.3 %shard_map.95 = (f32[8,1024]{1,0:T(8,128)S(1)}, f32[1]{0:T(128)}) custom-call(bf16[20,8,1024]{2,1,0:T(8,128)(2,1)S(1)} %bitcast.14, bf16[20,8,1024]{2,1,0:T(8,128)(2,1)S(1)} %bitcast.15, bf16[8,4,1024]{2,1,0:T(4,128)(2,1)S(1)} %bitcast.16, bf16[8,1024]{1,0:T(8,128)(2,1)S(1)} %bitcast.18, bf16[4,20,20]{2,1,0:T(8,128)(2,1)S(1)} %copy.11.mpo_ref, ...), custom_call_target="tpu_custom_call" | custom-call | tf_op jit(solution)/shard_map/pallas_call | solution.py:450
  79.2 0.6 copy.14
  (4 shorter events, 0.0 us)
Async XLA Ops:
  0.6 0.7 copy-start.7
  0.6 0.7 copy-start.6
  0.7 0.7 copy-start.5
  1.3 0.7 copy-start.4
  2.1 0.8 %copy-start.2 = (bf16[1,8,4,1024]{3,2,1,0:T(4,128)(2,1)S(1)}, bf16[1,8,4,1024]{3,2,1,0:T(4,128)(2,1)}, u32[]{:S(2)}) copy-start(bf16[1,8,4,1024]{3,2,1,0:T(4,128)(2,1)} %param.10) | copy-start | bytes 196612
  2.1 0.8 %copy-start.3 = (bf16[1,8,1024]{2,1,0:T(8,128)(2,1)S(1)}, bf16[1,8,1024]{2,1,0:T(8,128)(2,1)}, u32[]{:S(2)}) copy-start(bf16[1,8,1024]{2,1,0:T(8,128)(2,1)} %param.14) | copy-start | bytes 49156
  2.9 1.0 %copy-start = (bf16[8,20,1024]{2,0,1:T(8,128)(2,1)S(1)}, bf16[8,20,1024]{2,0,1:T(8,128)(2,1)}, u32[]{:S(2)}) copy-start(bf16[8,20,1024]{2,0,1:T(8,128)(2,1)} %param.8) | copy-start | bytes 983044
  3.9 1.0 %copy-start.1 = (bf16[1,8,20,1024]{3,1,2,0:T(8,128)(2,1)S(1)}, bf16[1,8,20,1024]{3,1,2,0:T(8,128)(2,1)}, u32[]{:S(2)}) copy-start(bf16[1,8,20,1024]{3,1,2,0:T(8,128)(2,1)} %param.15) | copy-start | bytes 983044

commit v4 on v3

--- a/solution.py
+++ b/solution.py
@@ -227,6 +227,24 @@
         )
 
     n_parts = len(parts)
+
+    def tensors_sent():
+        @pl.when(site < last)
+        def _():
+            for k in range(1, n_site):
+                t_copy(k, site).wait_send()
+
+    def sent(step):
+        for c in range(n_parts):
+            for k in range(n_high):
+                x_copy(step, c, k).wait_send()
+                if k > 0:
+                    rs_copy(step, c, k, high).wait_send()
+            for k in range(1, n_site):
+                @pl.when((step < last - 1) | (site_peer(k) == last))
+                def _():
+                    ag_copy(step, c, k, site).wait_send()
+
     order = list(range(1, n_high)) + [0]
 
     def chain_step(step, carry):
@@ -254,6 +272,11 @@
             prepare(step + 1)
 
         pl.when(step == 0)(prepare_right)
+
+        @pl.when(step > 0)
+        def _():
+            sent(step - 1)
+
         pl.when(step + 1 == last)(right_diagonal)
 
         totals = []
@@ -343,6 +366,12 @@
         for k in range(1, n_sector):
             red_copy(turn, k, member).start()
         redbuf[turn, member] = redout[turn]
+        if turn == 0:
+            tensors_sent()
+            sent(last - 1)
+        else:
+            for k in range(1, n_sector):
+                red_copy(turn - 1, k, member).wait_send()
         made = meanwhile() if meanwhile else None
         for k in range(1, n_sector):
             red_copy(turn, k, sector_peer(k)).wait_recv()
@@ -397,29 +426,10 @@
     for j in range(B * B // 128):
         kept = jnp.where((row & 31) == (col >> 5) + 4 * j, vector, 0.0)
         ground_ref[:, pl.ds(j * 128, 128)] = jnp.sum(kept.reshape(sec, B, 128), axis=1)
-    energy_ref[0] = energy[0, 0]
-
-    @pl.when(site < last)
-    def _():
-        for k in range(1, n_site):
-            t_copy(k, site).wait_send()
-
-    def sent(step, carry):
-        for c in range(n_parts):
-            for k in range(n_high):
-                x_copy(step, c, k).wait_send()
-                if k > 0:
-                    rs_copy(step, c, k, high).wait_send()
-            for k in range(1, n_site):
-                @pl.when((step < last - 1) | (site_peer(k) == last))
-                def _():
-                    ag_copy(step, c, k, site).wait_send()
-        return carry
-
-    lax.fori_loop(0, last, sent, 0)
-    for turn in range(DAV_ITERS + 1):
-        for k in range(1, n_sector):
-            red_copy(turn, k, member).wait_send()
+    energy_ref[...] = jnp.broadcast_to(energy, (8, 128))
+
+    for k in range(1, n_sector):
+        red_copy(DAV_ITERS, k, member).wait_send()
 
 
 def local(
@@ -436,7 +446,8 @@
     own = sec * dr
     cols = phys * own
     rows_a, wide = sec * B, bond * B
-    parts = tuple((at, min(256, wide - at)) for at in range(0, wide, 256))
+    cut = (wide // 128 + 1) // 2 * 128
+    parts = ((0, cut), (cut, wide - cut))
     n_parts = len(parts)
 
     target = route_owner[0, :, :, 0] * sec + route_sector[0]
@@ -451,10 +462,10 @@
         functools.partial(kernel, n_site, n_sector, sec, phys, bond, count_all, parts),
         out_shape=(
             jax.ShapeDtypeStruct((sec, B * B), F32),
-            jax.ShapeDtypeStruct((1,), F32),
+            jax.ShapeDtypeStruct((8, 128), F32),
         ),
         in_specs=[pl.BlockSpec(memory_space=pltpu.HBM if i < 2 else pltpu.VMEM) for i in range(7)],
-        out_specs=[pl.BlockSpec(memory_space=pltpu.VMEM), pl.BlockSpec(memory_space=pltpu.SMEM)],
+        out_specs=[pl.BlockSpec(memory_space=pltpu.VMEM), pl.BlockSpec(memory_space=pltpu.VMEM)],
         scratch_shapes=[
             pltpu.VMEM((phys, wide, wide), BF16),
             pltpu.VMEM((n_site, rows_a + 16, 128), BF16),
@@ -489,7 +500,7 @@
             collective_id=0, has_side_effects=True, vmem_limit_bytes=50 * 1024 * 1024
         ),
     )(env_in.transpose(1, 0, 2), right_env[0].transpose(1, 0, 2), site_tensors[0], psi[0], mpo_terms, goals, extent)
-    return ground[None], energy
+    return ground[None], energy[0, :1]
 
 
 def solution(mesh):

time: 82 us -> 79.3 us (0.967)
  between operations: 2.51 us -> 0.7 us
  Pallas kernels: 74.3 us -> 73 us
    pallas_call x1, Pallas kernels: 74.3 us -> 73 us  [local(): pl.pallas_call(functools.partial(kernel, n_site, n_sector, sec, phys, bon...]
where the time goes in v4:
time: 79.3 us; the launch traced here: 79 us
  Pallas kernels  73 us (92%)
  local copies, waits for them, and re-layouts  5.22 us (7%)
    pallas_call x1, Pallas kernels, local(): pl.pallas_call(functools.partial(kernel, n_site, n_sector, sec, phys, bon...  73 us
    unnamed x18, local copies, waits for them, and re-layouts  4.3 us

profile of v4, /device:TPU:0, one launch (start us, length us, event | category | flops | bytes accessed | tf_op | source)
XLA Modules:
  0.0 79.0 jit_solution(1954856448612957614)
XLA Ops:
  0.6 0.0 copy-start.7
  0.6 0.0 copy-start.6
  0.7 0.0 copy-start.5
  0.7 0.6 copy-done.7
  1.3 0.0 copy-done.6
  1.3 0.0 copy-done.5
  1.3 0.0 copy-start.4
  1.4 0.1 fusion
  1.4 0.1 broadcast_in_dim.20
  1.5 0.1 broadcast_in_dim.21
  1.6 0.1 broadcast_in_dim.19
  1.7 0.1 convert_element_type.17
  1.8 0.3 copy-done.4
  2.1 0.0 copy-start.2
  2.1 0.0 copy-start.3
  2.1 0.1 broadcast_in_dim.22.extent_ref
  2.2 0.7 copy-done.2
  2.9 0.0 copy-done.3
  2.9 0.0 copy-start
  2.9 1.0 %copy-done = bf16[8,20,1024]{2,0,1:T(8,128)(2,1)S(1)} copy-done((bf16[8,20,1024]{2,0,1:T(8,128)(2,1)S(1)}, bf16[8,20,1024]{2,0,1:T(8,128)(2,1)}, u32[]{:S(2)}) %copy-start) | copy-done | bytes 327704
  3.9 0.0 copy-start.1
  3.9 1.0 %copy-done.1 = bf16[1,8,20,1024]{3,1,2,0:T(8,128)(2,1)S(1)} copy-done((bf16[1,8,20,1024]{3,1,2,0:T(8,128)(2,1)S(1)}, bf16[1,8,20,1024]{3,1,2,0:T(8,128)(2,1)}, u32[]{:S(2)}) %copy-start.1) | copy-done | bytes 327704
  4.9 73.0 %shard_map.95 = (f32[8,1024]{1,0:T(8,128)S(1)}, f32[8,128]{1,0:T(8,128)S(1)}) custom-call(bf16[20,8,1024]{2,1,0:T(8,128)(2,1)S(1)} %bitcast.15, bf16[20,8,1024]{2,1,0:T(8,128)(2,1)S(1)} %bitcast.16, bf16[8,4,1024]{2,1,0:T(4,128)(2,1)S(1)} %bitcast.17, bf16[8,1024]{1,0:T(8,128)(2,1)S(1)} %bitcast.19, bf16[4,20,20]{2,1,0:T(8,128)(2,1)S(1)} %copy.11.mpo_ref, ...), custom_call_target="tpu_custom_call" | custom-call | tf_op jit(solution)/shard_map/pallas_call | solution.py:461
  77.9 0.5 slice.3
  78.4 0.6 copy.13
  (4 shorter events, 0.0 us)
Async XLA Ops:
  0.6 0.7 copy-start.7
  0.6 0.7 copy-start.6
  0.7 0.7 copy-start.5
  1.3 0.7 copy-start.4
  2.1 0.8 %copy-start.2 = (bf16[1,8,4,1024]{3,2,1,0:T(4,128)(2,1)S(1)}, bf16[1,8,4,1024]{3,2,1,0:T(4,128)(2,1)}, u32[]{:S(2)}) copy-start(bf16[1,8,4,1024]{3,2,1,0:T(4,128)(2,1)} %param.10) | copy-start | bytes 196612
  2.1 0.8 %copy-start.3 = (bf16[1,8,1024]{2,1,0:T(8,128)(2,1)S(1)}, bf16[1,8,1024]{2,1,0:T(8,128)(2,1)}, u32[]{:S(2)}) copy-start(bf16[1,8,1024]{2,1,0:T(8,128)(2,1)} %param.14) | copy-start | bytes 49156
  2.9 1.0 %copy-start = (bf16[8,20,1024]{2,0,1:T(8,128)(2,1)S(1)}, bf16[8,20,1024]{2,0,1:T(8,128)(2,1)}, u32[]{:S(2)}) copy-start(bf16[8,20,1024]{2,0,1:T(8,128)(2,1)} %param.8) | copy-start | bytes 983044
  3.9 1.0 %copy-start.1 = (bf16[1,8,20,1024]{3,1,2,0:T(8,128)(2,1)S(1)}, bf16[1,8,20,1024]{3,1,2,0:T(8,128)(2,1)}, u32[]{:S(2)}) copy-start(bf16[1,8,20,1024]{3,1,2,0:T(8,128)(2,1)} %param.15) | copy-start | bytes 983044
